TPU v7x, 32 devices: a whole 2x2x4 slice. The times are simulated.
32 devices in a mesh: groups: 2 (over y), dp: 4 (over z), tensor: 4 (over x, core).
Axes of the slice: x: 2, y: 2, z: 4, core: 2. Of those that a mesh axis runs over, the one named last changes fastest.
Arguments:
- inputs: bfloat16 [3, 32, 12288], P(None, ('groups', 'dp')), parts along dimension 1, may hold values from -6 to 6
- ln_gain: float32 [12288], replicated, may hold values from 0.1 to 1.9
- w_qkv: bfloat16 [3, 24, 12288, 128], P(None, 'tensor', 'dp'), may hold values from -0.0546875 to 0.0546875
- w_out: bfloat16 [24, 128, 12288], P('tensor', None, 'dp'), may hold values from -0.375 to 0.375
- key_cache: bfloat16 [32, 24, 128, 128], P(('groups', 'dp'), 'tensor'), parts along dimension 0, may hold values from -48 to 48
- value_cache: bfloat16 [32, 24, 128, 128], P(('groups', 'dp'), 'tensor'), parts along dimension 0, may hold values from -6 to 6
- cache_lens: int32 [32], P(('groups', 'dp')), parts along dimension 0, may hold values from 1 to 128, as said below
- active_heads: int32 [6, 8], P('groups'), parts along dimension 0, may hold values from 0 to 23, as said below
Outputs:
- attended: bfloat16 [3, 32, 12288], P(None, 'groups', ('dp', 'tensor')), parts along dimension 1
There are 2 independent parts, one for each index of `groups`. A program takes and returns all parts, laid end to end along the dimension named above; an argument that names none is the same for every part. Nothing has to cross between parts.
Inputs may be any that keep to these rules, and one draw needn't show every extreme that they name: `active_heads`: each step lists 8 distinct heads in increasing order; each aligned block of 6 heads holds at most 4 of them, and in every step some block holds exactly 4. `cache_lens`: some row has exactly 128 cached positions.
All inputs are finite; a program needn't handle non-finite values.
Results may differ from a plain program's by a relative error of at most 0.012.
The roundings to bfloat16 on the way count: a program that leaves them out, or rounds other values in their place, can miss the bound.
Values may be sent and summed in bfloat16 or wider, within the bound.
A program may use at most 64 MiB of HBM per device.

v0:
```python
import jax
import jax.numpy as jnp
from jax import lax
from jax.sharding import PartitionSpec as P

HEAD_CAP = 4


def normalize(rows, gain):
    values = rows.astype(jnp.float32)
    center = values - jnp.mean(values, axis=-1, keepdims=True)
    spread = jnp.mean(center * center, axis=-1, keepdims=True)
    return (center * lax.rsqrt(spread + 1e-05) * gain).astype(jnp.bfloat16)


def attend(
    queries,
    step_now,
    picked,
    alive_slots,
    new_keys,
    new_values,
    live_table,
    key_cache,
    value_cache,
    cache_lens,
):
    scale = queries.shape[-1] ** (-0.5)
    positions = jnp.arange(key_cache.shape[2], dtype=jnp.int32)
    old_valid = positions[None, :] < cache_lens[:, None]
    step_ids = jnp.arange(new_keys.shape[0], dtype=jnp.int32)
    results = []
    for slot in range(picked.shape[0]):
        head = picked[slot]
        keys_now = lax.dynamic_index_in_dim(key_cache, head, 1, keepdims=False)
        values_now = lax.dynamic_index_in_dim(value_cache, head, 1, keepdims=False)
        fresh_keys = lax.dynamic_index_in_dim(new_keys, head, 2, keepdims=False)
        fresh_values = lax.dynamic_index_in_dim(new_values, head, 2, keepdims=False)
        live_column = lax.dynamic_index_in_dim(live_table, head, 1, keepdims=False)
        query = queries[:, slot]
        old_scores = (
            jnp.einsum("bh,bph->bp", query, keys_now, preferred_element_type=jnp.float32) * scale
        )
        fresh_scores = (
            jnp.einsum("bh,jbh->bj", query, fresh_keys, preferred_element_type=jnp.float32) * scale
        )
        fresh_valid = ((step_ids <= step_now) & live_column)[None, :]
        top_score = jnp.maximum(
            jnp.max(jnp.where(old_valid, old_scores, -jnp.inf), axis=1),
            jnp.max(jnp.where(fresh_valid, fresh_scores, -jnp.inf), axis=1),
        )
        old_weight = jnp.where(old_valid, jnp.exp(old_scores - top_score[:, None]), 0.0)
        fresh_weight = jnp.where(fresh_valid, jnp.exp(fresh_scores - top_score[:, None]), 0.0)
        weight_sum = jnp.sum(old_weight, axis=1) + jnp.sum(fresh_weight, axis=1)
        old_prob = (old_weight / weight_sum[:, None]).astype(jnp.bfloat16)
        fresh_prob = (fresh_weight / weight_sum[:, None]).astype(jnp.bfloat16)
        blended = jnp.einsum("bp,bph->bh", old_prob, values_now, preferred_element_type=jnp.float32)
        blended = blended + jnp.einsum(
            "bj,jbh->bh", fresh_prob, fresh_values, preferred_element_type=jnp.float32
        )
        blended = jnp.where(alive_slots[slot], blended, 0.0)
        results.append(blended.astype(jnp.bfloat16))
    return jnp.stack(results, axis=1).reshape(queries.shape[0], -1)


def body(inputs, ln_gain, w_qkv, w_out, key_cache, value_cache, cache_lens, active_heads):
    step_count = inputs.shape[0]
    rows_here = inputs.shape[1]
    heads_here = w_qkv.shape[1]
    head_width = w_qkv.shape[3]
    local_ids = lax.axis_index("tensor") * heads_here + jnp.arange(heads_here, dtype=jnp.int32)
    live_table = jnp.any(active_heads[:, :, None] == local_ids[None, None, :], axis=1)
    ranking = (
        jnp.where(live_table, 0, heads_here) + jnp.arange(heads_here, dtype=jnp.int32)[None, :]
    )
    picked = jnp.argsort(ranking, axis=1)[:, :HEAD_CAP]
    alive_table = jnp.take_along_axis(live_table, picked, axis=1)
    slot_count = picked.shape[1]
    normed = normalize(inputs, ln_gain)
    new_keys = jnp.zeros((step_count, rows_here, heads_here, head_width), jnp.bfloat16)
    new_values = jnp.zeros((step_count, rows_here, heads_here, head_width), jnp.bfloat16)
    outputs = []
    for step_now in range(step_count):
        spread_rows = lax.all_to_all(
            normed[step_now], "dp", split_axis=1, concat_axis=0, tiled=True
        )
        pieces = []
        for project_slot in range(slot_count):
            project_block = lax.dynamic_index_in_dim(
                w_qkv, picked[step_now, project_slot], 1, keepdims=False
            )
            pieces.append(
                jnp.einsum(
                    "ri,sio->rso", spread_rows, project_block, preferred_element_type=jnp.float32
                )
            )
        summed = lax.psum_scatter(
            jnp.stack(pieces, axis=2).reshape(spread_rows.shape[0], -1),
            "dp",
            scatter_dimension=0,
            tiled=True,
        ).astype(jnp.bfloat16)
        attend_new_keys = new_keys
        attend_new_values = new_values
        split_proj = summed.reshape(rows_here, 3, slot_count, head_width)
        attend_new_keys = attend_new_keys.at[step_now].set(
            attend_new_keys[step_now].at[:, picked[step_now]].set(split_proj[:, 1])
        )
        attend_new_values = attend_new_values.at[step_now].set(
            attend_new_values[step_now].at[:, picked[step_now]].set(split_proj[:, 2])
        )
        blended = attend(
            split_proj[:, 0],
            step_now,
            picked[step_now],
            alive_table[step_now],
            attend_new_keys,
            attend_new_values,
            live_table,
            key_cache,
            value_cache,
            cache_lens,
        )
        blended, new_keys, new_values = (blended, attend_new_keys, attend_new_values)
        segment = lax.all_gather(blended, "dp", axis=0, tiled=True)
        total = None
        for slot in range(slot_count):
            block = lax.dynamic_index_in_dim(w_out, picked[step_now, slot], 0, keepdims=False)
            columns = segment[:, slot * head_width : (slot + 1) * head_width]
            term = jnp.dot(columns, block, preferred_element_type=jnp.float32)
            total = term if total is None else total + term
        outputs.append(
            lax.psum_scatter(total, "tensor", scatter_dimension=1, tiled=True).astype(jnp.bfloat16)
        )
    return jnp.stack(outputs)


def solution(mesh):
    placed = (
        P(None, ("groups", "dp"), None),
        P(),
        P(None, "tensor", "dp", None),
        P("tensor", None, "dp"),
        P(("groups", "dp"), "tensor", None, None),
        P(("groups", "dp"), "tensor", None, None),
        P(("groups", "dp")),
        P("groups", None),
    )
    return jax.shard_map(
        body,
        mesh=mesh,
        in_specs=placed,
        out_specs=P(None, "groups", ("dp", "tensor")),
        check_vma=False,
    )
```

profile of v0, /device:TPU:1, one launch (start us, length us, event | category | flops | bytes accessed | tf_op | source)
XLA Modules:
  0.0 234.5 jit_solution(13004624286980941782)
XLA Ops:
  6.5 1.3 convert_reduce_fusion
  7.8 1.3 fusion.101
  9.2 1.2 fusion.103
  10.4 0.8 fusion.443
  11.2 5.4 %all-to-all-start.1 = ((bf16[4,4,3072]{2,0,1:T(4,128)(2,1)}), bf16[4,4,3072]{2,0,1:T(4,128)(2,1)S(1)}, u32[]{:S(2)}, u32[]{:S(2)}) async-start(bf16[4,4,3072]{2,0,1:T(4,128)(2,1)} %bitcast.105), calls=%async_computation.2 | async-start | bytes 196608 | tf_op jit(solution)/shard_map/all_to_all | solution.py:84
  16.6 0.8 compare_reduce_fusion
  18.1 0.7 fusion.444
  34.4 0.7 gather_fusion
  43.4 1.2 dynamic-slice.46
  45.3 0.7 fusion.445
  46.0 4.5 %all-to-all-start = ((bf16[4,4,3072]{2,0,1:T(4,128)(2,1)}), bf16[4,4,3072]{2,0,1:T(4,128)(2,1)S(1)}, u32[]{:S(2)}, u32[]{:S(2)}) async-start(bf16[4,4,3072]{2,0,1:T(4,128)(2,1)} %bitcast.2), calls=%async_computation | async-start | bytes 196608 | tf_op jit(solution)/shard_map/all_to_all | solution.py:84
  50.5 2.1 fusion.48
  52.6 2.1 fusion.51
  54.7 2.1 fusion.54
  56.8 2.1 fusion.57
  58.9 4.5 %all-to-all-start.2 = ((bf16[4,4,3072]{2,0,1:T(4,128)(2,1)}), bf16[4,4,3072]{2,0,1:T(4,128)(2,1)S(1)}, u32[]{:S(2)}, u32[]{:S(2)}) async-start(bf16[4,4,3072]{2,0,1:T(4,128)(2,1)} %bitcast.208), calls=%async_computation.4 | async-start | bytes 196608 | tf_op jit(solution)/shard_map/all_to_all | solution.py:84
  63.5 2.1 fusion.39
  65.6 2.1 fusion.42
  67.7 2.1 fusion.45
  69.8 2.1 fusion.36
  71.9 2.1 fusion.63
  74.0 2.1 fusion.66
  76.1 2.2 fusion.60
  78.3 2.1 fusion.69
  80.7 20.1 %all-reduce.7 = (bf16[16,1536]{1,0:T(8,128)(2,1)S(1)}, bf16[16,1536]{1,0:T(8,128)(2,1)S(1)}, bf16[16,1536]{1,0:T(8,128)(2,1)S(1)}) all-reduce(f32[16,1536]{1,0:T(8,128)S(1)} %reshape.630, f32[16,1536]{1,0:T(8,128)S(1)} %reshape.620, f32[16,1536]{1,0:T(8,128)S(1)} %reshape.625), channel_id=6, replica_groups=mesh['groups'=2,'dp'=4,'tensor'=4] {'dp'}, use_global_device_ids=true, to_apply=%region_44.45.clone | all-reduce | flops 73728 | bytes 442368
  117.3 10.2 %all-gather = bf16[4,4,512]{2,1,0:T(4,128)(2,1)S(1)} all-gather(bf16[1,4,512]{2,1,0:T(4,128)(2,1)S(1)} %maximum_bitcast_fusion), channel_id=1, replica_groups=mesh['groups'=2,'dp'=4,'tensor'=4] {'dp'}, dimensions={0}, use_global_device_ids=true | all-gather | bytes 20480 | tf_op jit(solution)/shard_map/all_gather | solution.py:125
  127.5 1.4 fusion.85
  128.9 1.4 convolution_add_fusion.8
  130.2 1.4 convolution_add_fusion.7
  131.6 2.0 convolution_add_fusion.6
  136.0 0.7 fusion.385
  136.7 0.7 fusion.386
  138.0 10.2 %all-gather.1 = bf16[4,4,512]{2,1,0:T(4,128)(2,1)S(1)} all-gather(bf16[1,4,512]{2,1,0:T(4,128)(2,1)S(1)} %maximum_bitcast_fusion.1), channel_id=1, replica_groups=mesh['groups'=2,'dp'=4,'tensor'=4] {'dp'}, dimensions={0}, use_global_device_ids=true | all-gather | bytes 20480 | tf_op jit(solution)/shard_map/all_gather | solution.py:125
  148.2 1.4 fusion.80
  149.6 1.4 convolution_add_fusion.5
  151.0 1.4 convolution_add_fusion.4
  152.3 2.0 convolution_add_fusion.3
  157.4 0.7 fusion.389
  159.4 10.2 %all-gather.2 = bf16[4,4,512]{2,1,0:T(4,128)(2,1)S(1)} all-gather(bf16[1,4,512]{2,1,0:T(4,128)(2,1)S(1)} %maximum_bitcast_fusion.2), channel_id=1, replica_groups=mesh['groups'=2,'dp'=4,'tensor'=4] {'dp'}, dimensions={0}, use_global_device_ids=true | all-gather | bytes 20480 | tf_op jit(solution)/shard_map/all_gather | solution.py:125
  169.6 1.4 fusion.75
  171.0 1.4 convolution_add_fusion.2
  172.4 1.4 convolution_add_fusion.1
  173.8 2.0 convolution_add_fusion
  175.8 0.8 convert_bitcast_fusion.2
  176.6 27.7 %reduce-scatter.6.cloned.1.call-done = f32[16,768]{1,0:T(8,128)} async-done(((f32[16,3072]{1,0:T(8,128)}), f32[16,768]{1,0:T(8,128)}) %reduce-scatter.6.cloned.1.call-update) | async-done | bytes 49168 | tf_op jit(solution)/shard_map/reduce_scatter | solution.py:133
  204.4 0.8 convert_bitcast_fusion.1
  205.2 21.4 %reduce-scatter.8.cloned.1.call-done = f32[16,768]{1,0:T(8,128)} async-done(((f32[16,3072]{1,0:T(8,128)}), f32[16,768]{1,0:T(8,128)}) %reduce-scatter.8.cloned.1.call-update) | async-done | bytes 49168 | tf_op jit(solution)/shard_map/reduce_scatter | solution.py:133
  226.6 0.8 convert_bitcast_fusion
  (223 shorter events, 26.1 us)
Async XLA Ops:
  6.5 97.2 %copy-start = (bf16[4,6,128,128]{3,2,1,0:T(8,128)(2,1)S(1)}, bf16[4,6,128,128]{3,2,1,0:T(8,128)(2,1)}, u32[]{:S(2)}) copy-start(bf16[4,6,128,128]{3,2,1,0:T(8,128)(2,1)} %param.24) | copy-start | bytes 2359300
  11.2 34.8 %all-to-all-start.1 = ((bf16[4,4,3072]{2,0,1:T(4,128)(2,1)}), bf16[4,4,3072]{2,0,1:T(4,128)(2,1)S(1)}, u32[]{:S(2)}, u32[]{:S(2)}) async-start(bf16[4,4,3072]{2,0,1:T(4,128)(2,1)} %bitcast.105), calls=%async_computation.2 | async-start | bytes 196608 | tf_op jit(solution)/shard_map/all_to_all | solution.py:84
  46.0 12.9 %all-to-all-start = ((bf16[4,4,3072]{2,0,1:T(4,128)(2,1)}), bf16[4,4,3072]{2,0,1:T(4,128)(2,1)S(1)}, u32[]{:S(2)}, u32[]{:S(2)}) async-start(bf16[4,4,3072]{2,0,1:T(4,128)(2,1)} %bitcast.2), calls=%async_computation | async-start | bytes 196608 | tf_op jit(solution)/shard_map/all_to_all | solution.py:84
  58.9 12.9 %all-to-all-start.2 = ((bf16[4,4,3072]{2,0,1:T(4,128)(2,1)}), bf16[4,4,3072]{2,0,1:T(4,128)(2,1)S(1)}, u32[]{:S(2)}, u32[]{:S(2)}) async-start(bf16[4,4,3072]{2,0,1:T(4,128)(2,1)} %bitcast.208), calls=%async_computation.4 | async-start | bytes 196608 | tf_op jit(solution)/shard_map/all_to_all | solution.py:84
  63.5 112.4 %reduce-scatter.4.cloned.1.call-start = ((), (), s32[]{:S(2)}) async-start(), calls=%async_computation.6 | async-start | bytes 245760 | tf_op jit(solution)/shard_map/reduce_scatter | solution.py:133
  76.1 30.9 %copy-start.2 = (s32[4]{0:T(128)S(1)}, s32[4]{0:T(128)}, u32[]{:S(2)}) copy-start(s32[4]{0:T(128)} %param.26) | copy-start | bytes 52
  76.1 37.1 %copy-start.1 = (bf16[4,6,128,128]{3,2,1,0:T(8,128)(2,1)S(1)}, bf16[4,6,128,128]{3,2,1,0:T(8,128)(2,1)}, u32[]{:S(2)}) copy-start(bf16[4,6,128,128]{3,2,1,0:T(8,128)(2,1)} %param.25) | copy-start | bytes 2359300
  133.6 70.7 %reduce-scatter.6.cloned.1.call-start = ((), (), s32[]{:S(2)}) async-start(), calls=%async_computation.7 | async-start | bytes 245760 | tf_op jit(solution)/shard_map/reduce_scatter | solution.py:133
  172.3 54.2 %reduce-scatter.8.cloned.1.call-start = ((), (), s32[]{:S(2)}) async-start(), calls=%async_computation.8 | async-start | bytes 245760 | tf_op jit(solution)/shard_map/reduce_scatter | solution.py:133
Sparse Core Ops, SparseCore 0:
  133.8 26.3 reduce-scatter.3
  172.5 31.8 reduce-scatter.5
  206.8 19.7 reduce-scatter.7
where the time goes:
time: 237 us; the launch traced here: 235 us
  blocking collectives  50.8 us (21%)
  matrix products  50.3 us (21%)
  waiting for transfers between devices  49.2 us (21%)
  between operations  37.3 us (16%)
  other arithmetic  22.6 us (10%)
  starting transfers between devices  14.6 us (6%)
  local copies, waits for them, and re-layouts  9.71 us (4%)
    reduce_scatter x3, waiting for transfers between devices, body(): lax.psum_scatter(total, 'tensor', scatter_dimension=1, tiled=True)  49.2 us
    all_gather x3, blocking collectives, body(): segment = lax.all_gather(blended, 'dp', axis=0, tiled=True)  30.7 us
    dot_general x12, matrix products, body(): jnp.einsum('ri,sio->rso', spread_rows, project_block, preferred_element_t...  25.1 us
    unnamed x1, blocking collectives  20.1 us
    dot_general x12, matrix products, body(): term = jnp.dot(columns, block, preferred_element_type=jnp.float32)  18.3 us
    all_to_all x3, starting transfers between devices, body(): lax.all_to_all(normed[step_now], 'dp', split_axis=1, concat_axis=0, tiled...  14.5 us
    another operation x12, other arithmetic, attend(): return jnp.stack(results, axis=1).reshape(queries.shape[0], -1)  7.64 us
  transfers between devices with their start and end apart: 6, of which 2 were waited for; matrix products, arithmetic and copies ran while one was open for 19% of the time, Pallas kernels for 0%

commit v1 on v0

v1 whole, which is shorter than its diff:
```python
import functools

import jax
import jax.numpy as jnp
import numpy as np
from jax import lax
from jax.experimental import pallas as pl
from jax.experimental.pallas import tpu as pltpu
from jax.sharding import PartitionSpec as P

HEAD_CAP = 4
TILE = 16
MESH = pl.DeviceIdType.MESH


def kernel(
    dims,
    x_ref,
    gain_ref,
    perm_ref,
    lens_ref,
    active_ref,
    wqkv_hbm,
    wout_hbm,
    kc_hbm,
    vc_hbm,
    out_ref,
    wq,
    wo,
    kc,
    vc,
    rows32,
    nsend,
    xg,
    raw,
    packed,
    psend,
    precv,
    mg,
    osend,
    orecv,
    w_sem,
    c_sem,
    s1,
    r1,
    s2,
    r2,
    s3,
    r3,
    s4,
    r4,
):
    ndp, nt, heads, steps, rows, direct = dims
    hd = wq.shape[3]
    feats = wq.shape[2]
    cache = kc.shape[2]
    caps = HEAD_CAP
    spare = heads - caps
    me = lax.axis_index("dp")
    mt = lax.axis_index("tensor")
    f32, bf16 = jnp.float32, jnp.bfloat16

    weight_copies = []
    for t in range(3):
        for pair in range(heads // 2):
            c = pltpu.make_async_copy(
                wqkv_hbm.at[t, pl.ds(2 * pair, 2)],
                wq.at[t, pl.ds(2 * pair, 2)],
                w_sem.at[t * (heads // 2) + pair],
            )
            c.start()
            weight_copies.append(c)
    late = [
        pltpu.make_async_copy(kc_hbm, kc, c_sem.at[0]),
        pltpu.make_async_copy(vc_hbm, vc, c_sem.at[1]),
        pltpu.make_async_copy(wout_hbm, wo, c_sem.at[2]),
    ]
    for c in late:
        c.start()

    barrier = pltpu.get_barrier_semaphore()
    for k in range(1, ndp):
        pl.semaphore_signal(
            barrier, inc=1, device_id={"dp": lax.rem(me + k, ndp)}, device_id_type=MESH
        )
    if direct:
        for k in range(1, nt):
            pl.semaphore_signal(
                barrier, inc=1, device_id={"tensor": lax.rem(mt + k, nt)}, device_id_type=MESH
            )

    total = x_ref.shape[2]
    if TILE > steps * rows:
        rows32[...] = jnp.zeros_like(rows32)
    for s in range(steps):
        v = x_ref[s].astype(f32)
        center = v - jnp.sum(v, axis=-1, keepdims=True) * (1.0 / total)
        spread = jnp.sum(center * center, axis=-1, keepdims=True) * (1.0 / total)
        rows32[rows * s : rows * (s + 1), :] = center * lax.rsqrt(spread + 1e-05) * gain_ref[...]
    for p in range(ndp):
        nsend[p] = rows32[:, p * feats : (p + 1) * feats].astype(bf16)

    pl.semaphore_wait(barrier, ndp - 1 + (nt - 1 if direct else 0))

    def dp_copy(k, src, dst, send, recv):
        return pltpu.make_async_remote_copy(
            src_ref=src,
            dst_ref=dst,
            send_sem=send,
            recv_sem=recv,
            device_id={"dp": lax.rem(me + k, ndp)},
            device_id_type=MESH,
        )

    first = []
    for k in range(1, ndp):
        c = dp_copy(k, nsend.at[lax.rem(me + k, ndp)], xg.at[me], s1.at[k - 1], r1.at[k - 1])
        c.start()
        first.append(c)
    xg[me] = nsend[me]

    row = lax.broadcasted_iota(jnp.int32, (TILE, hd), 0)
    step_is = [(row >= rows * s) & (row < rows * (s + 1)) for s in range(steps)]
    row_is = []
    for r in range(rows):
        m = row == r
        for s in range(1, steps):
            m = m | (row == rows * s + r)
        row_is.append(m)
    live = []
    slot_of = []
    for s in range(steps):
        ids = [active_ref[s, a] for a in range(active_ref.shape[1])]
        flags, ranks = [], []
        seen = jnp.int32(0)
        for h in range(heads):
            hid = mt * heads + h
            f = jnp.int32(0)
            for i in ids:
                f = f + jnp.where(i == hid, jnp.int32(1), jnp.int32(0))
            flags.append(f)
            ranks.append(jnp.where(f > 0, jnp.maximum(seen, h - spare), jnp.int32(-1)))
            seen = seen + f
        live.append(flags)
        slot_of.append(ranks)
    rank_rows = []
    for h in range(heads):
        v = jnp.full((TILE, hd), -1, jnp.int32)
        for s in range(steps):
            v = jnp.where(step_is[s], slot_of[s][h], v)
        rank_rows.append(v)
    len_rows = jnp.full((TILE, cache), cache, jnp.int32)
    for r in range(rows):
        len_rows = jnp.where(row_is[r], lens_ref[r], len_rows)
    old_valid = lax.broadcasted_iota(jnp.int32, (TILE, cache), 1) < len_rows
    qrow = lax.broadcasted_iota(jnp.int32, (TILE, TILE), 0)
    kcol = lax.broadcasted_iota(jnp.int32, (TILE, TILE), 1)
    same = qrow == kcol
    for d in range(1, steps):
        same = same | (qrow - kcol == rows * d)
    same = same & (kcol < rows * steps)

    for c in first:
        c.wait_recv()

    second = [[], [], []]
    for t in range(3):
        for pair in range(heads // 2):
            weight_copies[t * (heads // 2) + pair].wait()

        @pl.loop(0, heads // 2)
        def _(pair):
            a = jnp.concatenate([wq[t, 2 * pair], wq[t, 2 * pair + 1]], axis=1)
            lhs = xg[...].reshape(ndp * TILE, feats)
            r = jnp.dot(lhs, a, preferred_element_type=f32)
            raw[2 * pair] = r[:, :hd].reshape(ndp, TILE, hd)
            raw[2 * pair + 1] = r[:, hd:].reshape(ndp, TILE, hd)

        for j in range(caps):
            acc = jnp.where((rank_rows[j] == j)[None], raw[j], 0.0)
            for h in range(j + 1, j + spare + 1):
                acc = jnp.where((rank_rows[h] == j)[None], raw[h], acc)
            packed[t, :, :, j * hd : (j + 1) * hd] = acc
            psend[t, :, :, j * hd : (j + 1) * hd] = acc.astype(bf16)
        for k in range(1, ndp):
            i = t * (ndp - 1) + k - 1
            c = dp_copy(k, psend.at[t, lax.rem(me + k, ndp)], precv.at[t, me], s2.at[i], r2.at[i])
            c.start()
            second[t].append(c)

    by_head = []
    for t in range(3):
        acc = packed[t, me]
        for k in range(1, ndp):
            second[t][k - 1].wait_recv()
            acc = acc + precv[t, lax.rem(me + ndp - k, ndp)].astype(f32)
        part = []
        for h in range(heads):
            v = jnp.zeros((TILE, hd), f32)
            for j in range(max(0, h - spare), min(caps, h + 1)):
                v = jnp.where(rank_rows[h] == j, acc[:, j * hd : (j + 1) * hd], v)
            part.append(v.astype(bf16))
        by_head.append(part)

    late[0].wait()
    late[1].wait()
    scale = hd ** (-0.5)
    nt_dims = (((1,), (1,)), ((), ()))
    for h in range(heads):
        q, kn, vn = by_head[0][h], by_head[1][h], by_head[2][h]
        wide = lax.dot_general(
            q, kc[:, h].reshape(rows * cache, hd), nt_dims, preferred_element_type=f32
        )
        old = wide[:, :cache]
        for r in range(1, rows):
            old = jnp.where(row_is[r], wide[:, r * cache : (r + 1) * cache], old)
        old = old * scale
        new = lax.dot_general(q, kn, nt_dims, preferred_element_type=f32) * scale
        alive = jnp.zeros((TILE, TILE), jnp.int32)
        for s in range(steps):
            alive = jnp.where((kcol >= rows * s) & (kcol < rows * (s + 1)), live[s][h], alive)
        new_valid = same & (alive > 0)
        top = jnp.maximum(
            jnp.max(jnp.where(old_valid, old, -jnp.inf), axis=1, keepdims=True),
            jnp.max(jnp.where(new_valid, new, -jnp.inf), axis=1, keepdims=True),
        )
        old_w = jnp.where(old_valid, jnp.exp(old - top), 0.0)
        new_w = jnp.where(new_valid, jnp.exp(new - top), 0.0)
        norm = jnp.sum(old_w, axis=1, keepdims=True) + jnp.sum(new_w, axis=1, keepdims=True)
        old_p = old_w / norm
        new_p = (new_w / norm).astype(bf16)
        spread_p = jnp.concatenate(
            [jnp.where(row_is[r], old_p, 0.0).astype(bf16) for r in range(rows)], axis=1
        )
        mixed = jnp.dot(
            spread_p, vc[:, h].reshape(rows * cache, hd), preferred_element_type=f32
        ) + jnp.dot(new_p, vn, preferred_element_type=f32)
        mixed = jnp.where(rank_rows[h] >= 0, mixed, 0.0)
        mg[me, :, h * hd : (h + 1) * hd] = mixed.astype(bf16)
    third = []
    for k in range(1, ndp):
        c = dp_copy(k, mg.at[me], mg.at[me], s3.at[k - 1], r3.at[k - 1])
        c.start()
        third.append(c)
    late[2].wait()
    for c in third:
        c.wait_recv()

    gathered = mg[...].reshape(ndp * TILE, heads * hd)
    lhs = jnp.dot(perm_ref[...], gathered, preferred_element_type=f32).astype(bf16)
    if direct:
        cols = feats // nt

        def block(c):
            w = wo[:, :, pl.ds(pl.multiple_of(c * cols, cols), cols)].reshape(heads * hd, cols)
            return jnp.dot(lhs, w, preferred_element_type=f32)

        fourth = []
        order = [nt // 2] + [k for k in range(1, nt) if k != nt // 2]
        for k in order:
            peer = lax.rem(mt + k, nt)
            osend[k - 1] = block(peer).astype(bf16)
            c = pltpu.make_async_remote_copy(
                src_ref=osend.at[k - 1],
                dst_ref=orecv.at[k - 1],
                send_sem=s4.at[k - 1],
                recv_sem=r4.at[k - 1],
                device_id={"tensor": peer},
                device_id_type=MESH,
            )
            c.start()
            fourth.append((k, c))
        acc = block(mt)
        for k, c in reversed(fourth):
            c.wait_recv()
            acc = acc + orecv[k - 1].astype(f32)
        out_ref[...] = acc.astype(out_ref.dtype)
        for k, c in fourth:
            c.wait_send()
    else:
        out_ref[...] = jnp.dot(
            lhs, wo[...].reshape(heads * hd, feats), preferred_element_type=f32
        )
    for c in first + second[0] + second[1] + second[2] + third:
        c.wait_send()


def body(inputs, ln_gain, w_qkv, w_out, key_cache, value_cache, cache_lens, active_heads):
    steps, rows, total = inputs.shape
    heads, feats, hd = w_qkv.shape[1:]
    ndp, nt = lax.axis_size("dp"), lax.axis_size("tensor")
    direct = (feats // nt) % 128 == 0
    count = steps * ndp * rows
    perm = np.zeros((count, ndp * TILE), np.float32)
    for s in range(steps):
        for p in range(ndp):
            for r in range(rows):
                perm[(s * ndp + p) * rows + r, p * TILE + s * rows + r] = 1.0
    bf16, f32 = jnp.bfloat16, jnp.float32
    cols = feats // nt if direct else 128
    orows = count if direct else TILE
    vmem = pl.BlockSpec(memory_space=pltpu.VMEM)
    smem = pl.BlockSpec(memory_space=pltpu.SMEM)
    hbm = pl.BlockSpec(memory_space=pl.ANY)
    dma = pltpu.SemaphoreType.DMA
    out = pl.pallas_call(
        functools.partial(kernel, (ndp, nt, heads, steps, rows, direct)),
        out_shape=jax.ShapeDtypeStruct((count, cols if direct else feats), bf16 if direct else f32),
        in_specs=[vmem, vmem, vmem, smem, smem, hbm, hbm, hbm, hbm],
        out_specs=vmem,
        scratch_shapes=[
            pltpu.VMEM(w_qkv.shape, bf16),
            pltpu.VMEM(w_out.shape, bf16),
            pltpu.VMEM(key_cache.shape, bf16),
            pltpu.VMEM(value_cache.shape, bf16),
            pltpu.VMEM((TILE, total), f32),
            pltpu.VMEM((ndp, TILE, feats), bf16),
            pltpu.VMEM((ndp, TILE, feats), bf16),
            pltpu.VMEM((heads, ndp, TILE, hd), f32),
            pltpu.VMEM((3, ndp, TILE, HEAD_CAP * hd), f32),
            pltpu.VMEM((3, ndp, TILE, HEAD_CAP * hd), bf16),
            pltpu.VMEM((3, ndp, TILE, HEAD_CAP * hd), bf16),
            pltpu.VMEM((ndp, TILE, heads * hd), bf16),
            pltpu.VMEM((nt - 1, orows, cols), bf16),
            pltpu.VMEM((nt - 1, orows, cols), bf16),
            dma((3 * (heads // 2),)),
            dma((3,)),
            dma((ndp - 1,)),
            dma((ndp - 1,)),
            dma((3 * (ndp - 1),)),
            dma((3 * (ndp - 1),)),
            dma((ndp - 1,)),
            dma((ndp - 1,)),
            dma((nt - 1,)),
            dma((nt - 1,)),
        ],
        compiler_params=pltpu.CompilerParams(
            collective_id=0, has_side_effects=True, vmem_limit_bytes=56 * 1024 * 1024
        ),
    )(
        inputs,
        ln_gain.reshape(1, total),
        jnp.asarray(perm, bf16),
        cache_lens,
        active_heads,
        w_qkv,
        w_out,
        key_cache,
        value_cache,
    )
    if not direct:
        out = lax.psum_scatter(out, "tensor", scatter_dimension=1, tiled=True).astype(bf16)
    return out.reshape(steps, ndp * rows, -1)


def solution(mesh):
    placed = (
        P(None, ("groups", "dp"), None),
        P(),
        P(None, "tensor", "dp", None),
        P("tensor", None, "dp"),
        P(("groups", "dp"), "tensor", None, None),
        P(("groups", "dp"), "tensor", None, None),
        P(("groups", "dp")),
        P("groups", None),
    )
    return jax.shard_map(
        body,
        mesh=mesh,
        in_specs=placed,
        out_specs=P(None, "groups", ("dp", "tensor")),
        check_vma=False,
    )
```

time: 237 us -> 36 us (0.15)
  blocking collectives: 50.8 us -> 0 us
  matrix products: 50.3 us -> 0 us
  waiting for transfers between devices: 49.2 us -> 0 us
  between operations: 37.3 us -> 0.01 us
  Pallas kernels: 0 us -> 34.3 us
  other arithmetic: 22.6 us -> 0 us
  starting transfers between devices: 14.6 us -> 0 us
  local copies, waits for them, and re-layouts: 9.71 us -> 1.52 us
    dot_general x72 -> x0, matrix products: 50.3 us -> none  [the longest x12 25.1 us: body(): jnp.einsum('ri,sio->rso', spread_rows, project_block, preferred_element_t...]
    reduce_scatter x3 -> x0, waiting for transfers between devices: 49.2 us -> none  [body(): lax.psum_scatter(total, 'tensor', scatter_dimension=1, tiled=True)]
    pallas_call x0 -> x1, Pallas kernels: none -> 34.3 us  [body(): pl.pallas_call(functools.partial(kernel, (ndp, nt, heads, steps, rows, di...]
    all_gather x3 -> x0, blocking collectives: 30.7 us -> none  [body(): segment = lax.all_gather(blended, 'dp', axis=0, tiled=True)]
    unnamed x1 -> x0, blocking collectives: 20.1 us -> none
    all_to_all x3 -> x0, starting transfers between devices: 14.5 us -> none  [body(): lax.all_to_all(normed[step_now], 'dp', split_axis=1, concat_axis=0, tiled...]
    another operation x19 -> x0, other arithmetic: 10.7 us -> none  [the longest x12 7.64 us: attend(): return jnp.stack(results, axis=1).reshape(queries.shape[0], -1)]
    reduce_sum x16 -> x0, other arithmetic: 5.38 us -> none  [the longest x14 2.77 us: attend(): weight_sum = jnp.sum(old_weight, axis=1) + jnp.sum(fresh_weight, axis=1)]
  transfers between devices with their start and end apart: 6 -> 0, of which waited for: 2 -> 0; matrix products, arithmetic and copies ran while one was open for 19% -> 0% of each run, Pallas kernels for 0% -> 0%
where the time goes in v1:
time: 36 us; the launch traced here: 35.8 us
  Pallas kernels  34.3 us (95%)
  local copies, waits for them, and re-layouts  1.52 us (4%)
    pallas_call x1, Pallas kernels, body(): pl.pallas_call(functools.partial(kernel, (ndp, nt, heads, steps, rows, di...  34.3 us
    unnamed x1, local copies, waits for them, and re-layouts  1.52 us

profile of v1, /device:TPU:1, one launch (start us, length us, event | category | flops | bytes accessed | tf_op | source)
XLA Modules:
  0.0 35.8 jit_solution(17197743298301900604)
XLA Ops:
  0.0 34.3 %shard_map.91 = bf16[48,768]{1,0:T(8,128)(2,1)} custom-call(bf16[3,4,12288]{2,1,0:T(4,128)(2,1)} %x_ref.1, f32[1,12288]{1,0:T(1,128)} %bitcast.3, bf16[48,64]{1,0:T(8,128)(2,1)} %constant.2.clone.perm_ref, s32[4]{0:T(128)} %lens_ref.1, s32[3,8]{1,0:T(4,128)} %active_ref.1, bf16[3,6,3072,128]{3,2,1,0:T(8,128)(2,1)} %wqkv_hbm.1, ...), custom_call_target="tpu_custom_call" | custom-call | tf_op jit(solution)/shard_map/pallas_call | solution.py:306
  34.3 1.5 %copy.11 = bf16[3,16,768]{2,1,0:T(8,128)(2,1)} copy(bf16[3,16,768]{2,1,0:T(8,128)(2,1)} %bitcast.2) | data formatting | bytes 147456

commit v2 on v1

--- a/solution.py
+++ b/solution.py
@@ -49,6 +49,8 @@
     r3,
     s4,
     r4,
+    s5,
+    r5,
 ):
     ndp, nt, heads, steps, rows, direct = dims
     hd = wq.shape[3]
@@ -97,8 +99,16 @@
         center = v - jnp.sum(v, axis=-1, keepdims=True) * (1.0 / total)
         spread = jnp.sum(center * center, axis=-1, keepdims=True) * (1.0 / total)
         rows32[rows * s : rows * (s + 1), :] = center * lax.rsqrt(spread + 1e-05) * gain_ref[...]
-    for p in range(ndp):
-        nsend[p] = rows32[:, p * feats : (p + 1) * feats].astype(bf16)
+    halves, _, _, width = xg.shape
+    core = lax.rem(mt, 2)
+    sibling = mt + 1 - 2 * core
+    mine = core if halves == 2 else 0
+
+    def columns(p, half):
+        return rows32[:, pl.ds(pl.multiple_of(p * feats + half * width, 128), width)].astype(bf16)
+
+    for k in range(1, ndp):
+        nsend[k - 1] = columns(lax.rem(me + k, ndp), mine)
 
     pl.semaphore_wait(barrier, ndp - 1 + (nt - 1 if direct else 0))
 
@@ -114,10 +124,11 @@
 
     first = []
     for k in range(1, ndp):
-        c = dp_copy(k, nsend.at[lax.rem(me + k, ndp)], xg.at[me], s1.at[k - 1], r1.at[k - 1])
+        c = dp_copy(k, nsend.at[k - 1], xg.at[mine, me], s1.at[k - 1], r1.at[k - 1])
         c.start()
         first.append(c)
-    xg[me] = nsend[me]
+    for half in range(halves):
+        xg[half, me] = columns(me, half)
 
     row = lax.broadcasted_iota(jnp.int32, (TILE, hd), 0)
     step_is = [(row >= rows * s) & (row < rows * (s + 1)) for s in range(steps)]
@@ -160,21 +171,64 @@
         same = same | (qrow - kcol == rows * d)
     same = same & (kcol < rows * steps)
 
-    for c in first:
-        c.wait_recv()
+    shared = []
+    for k in range(1, ndp):
+        first[k - 1].wait_recv()
+        if halves == 2:
+            piece = xg.at[core, lax.rem(me + ndp - k, ndp)]
+            c = pltpu.make_async_remote_copy(
+                src_ref=piece,
+                dst_ref=piece,
+                send_sem=s5.at[k - 1],
+                recv_sem=r5.at[k - 1],
+                device_id={"tensor": sibling},
+                device_id_type=MESH,
+            )
+            c.start()
+            shared.append(c)
+
+    def project(t, pair, half):
+        depth = pl.ds(pl.multiple_of(half * width, 128), width)
+        a = jnp.concatenate([wq[t, 2 * pair, depth], wq[t, 2 * pair + 1, depth]], axis=1)
+        lhs = xg[half].reshape(ndp * TILE, width)
+        return jnp.dot(lhs, a, preferred_element_type=f32)
+
+    def keep(pair, r):
+        raw[2 * pair] = r[:, :hd].reshape(ndp, TILE, hd)
+        raw[2 * pair + 1] = r[:, hd:].reshape(ndp, TILE, hd)
 
     second = [[], [], []]
     for t in range(3):
         for pair in range(heads // 2):
             weight_copies[t * (heads // 2) + pair].wait()
 
-        @pl.loop(0, heads // 2)
-        def _(pair):
-            a = jnp.concatenate([wq[t, 2 * pair], wq[t, 2 * pair + 1]], axis=1)
-            lhs = xg[...].reshape(ndp * TILE, feats)
-            r = jnp.dot(lhs, a, preferred_element_type=f32)
-            raw[2 * pair] = r[:, :hd].reshape(ndp, TILE, hd)
-            raw[2 * pair + 1] = r[:, hd:].reshape(ndp, TILE, hd)
+        if t == 0 and halves == 2:
+
+            @pl.loop(0, heads // 2)
+            def _(pair):
+                keep(pair, project(t, pair, core))
+
+            for c in shared:
+                c.wait_recv()
+
+            @pl.loop(0, heads // 2)
+            def _(pair):
+                r = project(t, pair, 1 - core)
+                keep(
+                    pair,
+                    r
+                    + jnp.concatenate(
+                        [raw[2 * pair + i].reshape(ndp * TILE, hd) for i in range(2)], axis=1
+                    ),
+                )
+        else:
+
+            @pl.loop(0, heads // 2)
+            def _(pair):
+                r = project(t, pair, 0)
+                for half in range(1, halves):
+                    r = r + project(t, pair, half)
+                keep(pair, r)
 
         for j in range(caps):
             acc = jnp.where((rank_rows[j] == j)[None], raw[j], 0.0)
@@ -188,8 +242,7 @@
             c.start()
             second[t].append(c)
 
-    by_head = []
-    for t in range(3):
+    def reduced(t):
         acc = packed[t, me]
         for k in range(1, ndp):
             second[t][k - 1].wait_recv()
@@ -200,22 +253,27 @@
             for j in range(max(0, h - spare), min(caps, h + 1)):
                 v = jnp.where(rank_rows[h] == j, acc[:, j * hd : (j + 1) * hd], v)
             part.append(v.astype(bf16))
-        by_head.append(part)
+        return part
 
     late[0].wait()
     late[1].wait()
+    queries = reduced(0)
     scale = hd ** (-0.5)
     nt_dims = (((1,), (1,)), ((), ()))
+    olds = []
     for h in range(heads):
-        q, kn, vn = by_head[0][h], by_head[1][h], by_head[2][h]
         wide = lax.dot_general(
-            q, kc[:, h].reshape(rows * cache, hd), nt_dims, preferred_element_type=f32
+            queries[h], kc[:, h].reshape(rows * cache, hd), nt_dims, preferred_element_type=f32
         )
         old = wide[:, :cache]
         for r in range(1, rows):
             old = jnp.where(row_is[r], wide[:, r * cache : (r + 1) * cache], old)
-        old = old * scale
-        new = lax.dot_general(q, kn, nt_dims, preferred_element_type=f32) * scale
+        olds.append(old * scale)
+    new_keys = reduced(1)
+    probs = []
+    for h in range(heads):
+        old = olds[h]
+        new = lax.dot_general(queries[h], new_keys[h], nt_dims, preferred_element_type=f32) * scale
         alive = jnp.zeros((TILE, TILE), jnp.int32)
         for s in range(steps):
             alive = jnp.where((kcol >= rows * s) & (kcol < rows * (s + 1)), live[s][h], alive)
@@ -232,11 +290,20 @@
         spread_p = jnp.concatenate(
             [jnp.where(row_is[r], old_p, 0.0).astype(bf16) for r in range(rows)], axis=1
         )
-        mixed = jnp.dot(
+        cached = jnp.dot(
             spread_p, vc[:, h].reshape(rows * cache, hd), preferred_element_type=f32
-        ) + jnp.dot(new_p, vn, preferred_element_type=f32)
-        mixed = jnp.where(rank_rows[h] >= 0, mixed, 0.0)
-        mg[me, :, h * hd : (h + 1) * hd] = mixed.astype(bf16)
+        )
+        probs.append((cached, new_p))
+    new_values = reduced(2)
+    mixed = []
+    for h in range(heads):
+        cached, new_p = probs[h]
+        mixed.append(cached + jnp.dot(new_p, new_values[h], preferred_element_type=f32))
+    for j in range(caps):
+        acc = jnp.where(rank_rows[j] == j, mixed[j], 0.0)
+        for h in range(j + 1, j + spare + 1):
+            acc = jnp.where(rank_rows[h] == j, mixed[h], acc)
+        mg[me, :, j * hd : (j + 1) * hd] = acc.astype(bf16)
     third = []
     for k in range(1, ndp):
         c = dp_copy(k, mg.at[me], mg.at[me], s3.at[k - 1], r3.at[k - 1])
@@ -246,8 +313,21 @@
     for c in third:
         c.wait_recv()
 
-    gathered = mg[...].reshape(ndp * TILE, heads * hd)
-    lhs = jnp.dot(perm_ref[...], gathered, preferred_element_type=f32).astype(bf16)
+    gathered = mg[...].reshape(ndp * TILE, caps * hd)
+    ordered = jnp.dot(perm_ref[...], gathered, preferred_element_type=f32)
+    group = ndp * rows
+    by_step = []
+    for s in range(steps):
+        here = ordered[s * group : (s + 1) * group]
+        part = []
+        for h in range(heads):
+            slot = jnp.full((group, hd), slot_of[s][h], jnp.int32)
+            v = jnp.zeros((group, hd), f32)
+            for j in range(max(0, h - spare), min(caps, h + 1)):
+                v = jnp.where(slot == j, here[:, j * hd : (j + 1) * hd], v)
+            part.append(v)
+        by_step.append(jnp.concatenate(part, axis=1))
+    lhs = jnp.concatenate(by_step, axis=0).astype(bf16)
     if direct:
         cols = feats // nt
 
@@ -256,9 +336,11 @@
             return jnp.dot(lhs, w, preferred_element_type=f32)
 
         fourth = []
-        order = [nt // 2] + [k for k in range(1, nt) if k != nt // 2]
-        for k in order:
-            peer = lax.rem(mt + k, nt)
+        partners = []
+        for k in range(2, nt, 2):
+            partners += [lax.rem(mt + k, nt), lax.rem(sibling + k, nt)]
+        partners.append(sibling)
+        for k, peer in enumerate(partners, 1):
             osend[k - 1] = block(peer).astype(bf16)
             c = pltpu.make_async_remote_copy(
                 src_ref=osend.at[k - 1],
@@ -281,7 +363,7 @@
         out_ref[...] = jnp.dot(
             lhs, wo[...].reshape(heads * hd, feats), preferred_element_type=f32
         )
-    for c in first + second[0] + second[1] + second[2] + third:
+    for c in first + shared + second[0] + second[1] + second[2] + third:
         c.wait_send()
 
 
@@ -290,6 +372,7 @@
     heads, feats, hd = w_qkv.shape[1:]
     ndp, nt = lax.axis_size("dp"), lax.axis_size("tensor")
     direct = (feats // nt) % 128 == 0
+    halves = 2 if direct and (feats // 2) % 128 == 0 else 1
     count = steps * ndp * rows
     perm = np.zeros((count, ndp * TILE), np.float32)
     for s in range(steps):
@@ -314,13 +397,13 @@
             pltpu.VMEM(key_cache.shape, bf16),
             pltpu.VMEM(value_cache.shape, bf16),
             pltpu.VMEM((TILE, total), f32),
-            pltpu.VMEM((ndp, TILE, feats), bf16),
-            pltpu.VMEM((ndp, TILE, feats), bf16),
+            pltpu.VMEM((ndp - 1, TILE, feats // halves), bf16),
+            pltpu.VMEM((halves, ndp, TILE, feats // halves), bf16),
             pltpu.VMEM((heads, ndp, TILE, hd), f32),
             pltpu.VMEM((3, ndp, TILE, HEAD_CAP * hd), f32),
             pltpu.VMEM((3, ndp, TILE, HEAD_CAP * hd), bf16),
             pltpu.VMEM((3, ndp, TILE, HEAD_CAP * hd), bf16),
-            pltpu.VMEM((ndp, TILE, heads * hd), bf16),
+            pltpu.VMEM((ndp, TILE, HEAD_CAP * hd), bf16),
             pltpu.VMEM((nt - 1, orows, cols), bf16),
             pltpu.VMEM((nt - 1, orows, cols), bf16),
             dma((3 * (heads // 2),)),
@@ -333,6 +416,8 @@
             dma((ndp - 1,)),
             dma((nt - 1,)),
             dma((nt - 1,)),
+            dma((ndp - 1,)),
+            dma((ndp - 1,)),
         ],
         compiler_params=pltpu.CompilerParams(
             collective_id=0, has_side_effects=True, vmem_limit_bytes=56 * 1024 * 1024

time: 36 us -> 30.8 us (0.86)
  Pallas kernels: 34.3 us -> 29.1 us
    pallas_call x1, Pallas kernels: 34.3 us -> 29.1 us  [body(): pl.pallas_call(functools.partial(kernel, (ndp, nt, heads, steps, rows, di...]
where the time goes in v2:
time: 30.8 us; the launch traced here: 30.7 us
  Pallas kernels  29.1 us (94%)
  local copies, waits for them, and re-layouts  1.52 us (5%)
    pallas_call x1, Pallas kernels, body(): pl.pallas_call(functools.partial(kernel, (ndp, nt, heads, steps, rows, di...  29.1 us
    unnamed x1, local copies, waits for them, and re-layouts  1.52 us

profile of v2, /device:TPU:1, one launch (start us, length us, event | category | flops | bytes accessed | tf_op | source)
XLA Modules:
  0.0 30.7 jit_solution(14587063684400084822)
XLA Ops:
  0.0 29.1 %shard_map.91 = bf16[48,768]{1,0:T(8,128)(2,1)} custom-call(bf16[3,4,12288]{2,1,0:T(4,128)(2,1)} %x_ref.1, f32[1,12288]{1,0:T(1,128)} %bitcast.3, bf16[48,64]{1,0:T(8,128)(2,1)} %constant.2.clone.perm_ref, s32[4]{0:T(128)} %lens_ref.1, s32[3,8]{1,0:T(4,128)} %active_ref.1, bf16[3,6,3072,128]{3,2,1,0:T(8,128)(2,1)} %wqkv_hbm.1, ...), custom_call_target="tpu_custom_call" | custom-call | tf_op jit(solution)/shard_map/pallas_call | solution.py:389
  29.1 1.5 %copy.11 = bf16[3,16,768]{2,1,0:T(8,128)(2,1)} copy(bf16[3,16,768]{2,1,0:T(8,128)(2,1)} %bitcast.2) | data formatting | bytes 147456

commit v3 on v2

--- a/solution.py
+++ b/solution.py
@@ -204,15 +204,13 @@
 
         if t == 0 and halves == 2:
 
-            @pl.loop(0, heads // 2)
-            def _(pair):
+            for pair in range(heads // 2):
                 keep(pair, project(t, pair, core))
 
             for c in shared:
                 c.wait_recv()
 
-            @pl.loop(0, heads // 2)
-            def _(pair):
+            for pair in range(heads // 2):
                 r = project(t, pair, 1 - core)
                 keep(
                     pair,
@@ -223,8 +221,7 @@
                 )
         else:
 
-            @pl.loop(0, heads // 2)
-            def _(pair):
+            for pair in range(heads // 2):
                 r = project(t, pair, 0)
                 for half in range(1, halves):
                     r = r + project(t, pair, half)

time: 30.8 us -> 30.4 us (0.987)
  Pallas kernels: 29.1 us -> 28.7 us
    pallas_call x1, Pallas kernels: 29.1 us -> 28.7 us  [body(): pl.pallas_call(functools.partial(kernel, (ndp, nt, heads, steps, rows, di...]
where the time goes in v3:
time: 30.4 us; the launch traced here: 30.2 us
  Pallas kernels  28.7 us (94%)
  local copies, waits for them, and re-layouts  1.52 us (5%)
    pallas_call x1, Pallas kernels, body(): pl.pallas_call(functools.partial(kernel, (ndp, nt, heads, steps, rows, di...  28.7 us
    unnamed x1, local copies, waits for them, and re-layouts  1.52 us

profile of v3, /device:TPU:1, one launch (start us, length us, event | category | flops | bytes accessed | tf_op | source)
XLA Modules:
  0.0 30.2 jit_solution(3974801237852193978)
XLA Ops:
  0.0 28.7 %shard_map.91 = bf16[48,768]{1,0:T(8,128)(2,1)} custom-call(bf16[3,4,12288]{2,1,0:T(4,128)(2,1)} %x_ref.1, f32[1,12288]{1,0:T(1,128)} %bitcast.3, bf16[48,64]{1,0:T(8,128)(2,1)} %constant.2.clone.perm_ref, s32[4]{0:T(128)} %lens_ref.1, s32[3,8]{1,0:T(4,128)} %active_ref.1, bf16[3,6,3072,128]{3,2,1,0:T(8,128)(2,1)} %wqkv_hbm.1, ...), custom_call_target="tpu_custom_call" | custom-call | tf_op jit(solution)/shard_map/pallas_call | solution.py:386
  28.7 1.5 %copy.11 = bf16[3,16,768]{2,1,0:T(8,128)(2,1)} copy(bf16[3,16,768]{2,1,0:T(8,128)(2,1)} %bitcast.2) | data formatting | bytes 147456
